TPU v7x, 32 devices: a whole 2x2x4 slice. The times are simulated.
32 devices in a mesh: gx: 4 (over z), gy: 2 (over y), gz: 4 (over x, core).
Axes of the slice: x: 2, y: 2, z: 4, core: 2. Of those that a mesh axis runs over, the one named last changes fastest.
Arguments:
- grad_out: bfloat16 [64, 32, 16, 64], P(None, 'gx', 'gy', 'gz'), may hold values from -6 to 6
- features: bfloat16 [64, 32, 16, 64], P(None, 'gx', 'gy', 'gz'), may hold values from -6 to 6
- brick_mask: int32 [4, 2, 8], P('gx', 'gy', 'gz'), may hold values 0 or 1
- voxel_mask: int32 [32, 16, 64], P('gx', 'gy', 'gz'), may hold values 0 or 1
- weight: bfloat16 [64, 1728], replicated, may hold values from -0.15625 to 0.15625
Outputs:
- grad_input: bfloat16 [64, 32, 16, 64], P(None, 'gx', 'gy', 'gz')
- grad_weight: float32 [64, 1728], replicated
All inputs are finite; a program needn't handle non-finite values. No bound on the sum of `brick_mask` or of `voxel_mask` on one device may be relied on, other than what follows from the above.
Results may differ from a plain program's by a relative error of at most 0.001.
Values may be sent and summed in bfloat16 or wider, within the bound.
A program may use at most 64 MiB of HBM per device.

v0:
```python
import math

import jax
import jax.numpy as jnp
from jax import lax
from jax.sharding import PartitionSpec as P

BRICK = 8


def extended(shard, sides, width):
    for axis, dim in sides:
        peers, length = (lax.axis_size(axis), shard.shape[dim])
        up = [(i, (i + 1) % peers) for i in range(peers - 1)]
        down = [(j, i) for i, j in up]
        last = lax.slice_in_dim(shard, length - width, length, axis=dim)
        initial = lax.slice_in_dim(shard, 0, width, axis=dim)
        before = lax.ppermute(last, axis, up)
        after = lax.ppermute(initial, axis, down)
        shard = jnp.concatenate([before, shard, after], axis=dim)
    return shard


def local(grad_out, features, brick_mask, voxel_mask, weight):
    chans, size_x, size_y, size_z = grad_out.shape
    count = size_x * size_y * size_z
    upsampled = jnp.repeat(jnp.repeat(jnp.repeat(brick_mask, BRICK, 0), BRICK, 1), BRICK, 2)
    active = upsampled * voxel_mask > 0
    masked_grad = jnp.where(active[None], grad_out, jnp.zeros_like(grad_out))
    masked_feat = jnp.where(active[None], features, jnp.zeros_like(features))
    feat_flat = masked_feat.reshape(chans, count)
    padded = extended(masked_grad, (("gx", 1), ("gy", 2), ("gz", 3)), 1)
    devices = lax.axis_size("gx") * lax.axis_size("gy") * lax.axis_size("gz")
    scale = 1.0 / math.sqrt(count * devices)
    total = jnp.zeros((chans, count), jnp.float32)
    planes = []
    for shift_x in (-1, 0, 1):
        pieces = []
        for shift_y in (-1, 0, 1):
            for shift_z in (-1, 0, 1):
                shifted = padded[
                    :,
                    1 - shift_x : 1 - shift_x + size_x,
                    1 - shift_y : 1 - shift_y + size_y,
                    1 - shift_z : 1 - shift_z + size_z,
                ]
                pieces.append(shifted.reshape(chans, count))
        columns = jnp.concatenate(pieces, axis=0)
        start = 9 * (shift_x + 1) * chans
        kernel_plane = weight[:, start : start + 9 * chans]
        total = total + jnp.dot(kernel_plane, columns, preferred_element_type=jnp.float32)
        plane_grad = lax.dot_general(
            feat_flat, columns, (((1,), (1,)), ((), ())), preferred_element_type=jnp.float32
        )
        planes.append(plane_grad)
    grad_weight = jnp.concatenate(planes, axis=1)
    grad_weight = lax.psum(grad_weight, ("gx", "gy", "gz"))
    grad_weight = grad_weight * scale
    grad_input = jnp.where(active.reshape(1, count), total, jnp.zeros_like(total)).astype(
        jnp.bfloat16
    )
    return (grad_input.reshape(chans, size_x, size_y, size_z), grad_weight)


def solution(mesh):
    return jax.shard_map(
        local,
        mesh=mesh,
        in_specs=(
            P(None, "gx", "gy", "gz"),
            P(None, "gx", "gy", "gz"),
            P("gx", "gy", "gz"),
            P("gx", "gy", "gz"),
            P(),
        ),
        out_specs=(P(None, "gx", "gy", "gz"), P()),
        check_vma=False,
    )
```

profile of v0, /device:TPU:0, one launch (start us, length us, event | category | flops | bytes accessed | tf_op | source)
XLA Modules:
  0.0 190.5 jit_solution(2308391098219094017)
XLA Ops:
  7.2 0.0 all-reduce.2.cloned.1.call-start
  7.2 0.7 broadcast_in_dim.35
  7.9 0.1 broadcast_in_dim.36
  8.0 0.8 multiply_compare_fusion
  8.8 1.2 broadcast_select_fusion
  10.0 1.3 collective-permute-start.1
  11.3 5.6 %collective-permute-start = (bf16[64,1,8,16]{0,3,2,1:T(8,128)(2,1)S(1)}, bf16[64,1,8,16]{0,3,2,1:T(8,128)(2,1)S(1)}, u32[]{:S(2)}, u32[]{:S(2)}) collective-permute-start(bf16[64,1,8,16]{0,3,2,1:T(8,128)(2,1)S(1)} %get-tuple-element.38), channel_id=1, source_target_pairs={{0,8},{8,16},{16,24},{1,9},{9,17},{17,25},{2,10},{10,18},{18,26},{... | collective-permute-start | bytes 49160 | tf_op jit(solution)/shard_map/ppermute | solution.py:18
  16.9 0.1 broadcast_in_dim.38
  17.0 0.0 collective-permute-done.1
  17.0 1.5 collective-permute-done
  18.5 1.3 collective-permute-start.3
  19.8 4.5 %collective-permute-start.2 = (bf16[64,10,1,16]{0,3,2,1:T(8,128)(2,1)S(1)}, bf16[64,10,1,16]{0,3,2,1:T(8,128)(2,1)S(1)}, u32[]{:S(2)}, u32[]{:S(2)}) collective-permute-start(bf16[64,10,1,16]{0,3,2,1:T(8,128)(2,1)S(1)} %get-tuple-element.34), channel_id=1, source_target_pairs={{0,4},{1,5},{2,6},{3,7},{8,12},{9,13},{10,14},{11,15},{16,20},{17,... | collective-permute-start | bytes 61448 | tf_op jit(solution)/shard_map/ppermute | solution.py:18
  24.4 0.9 pad_maximum_fusion.2
  25.2 0.0 collective-permute-done.3
  25.2 0.8 collective-permute-done.2
  26.0 0.1 pad_maximum_fusion.4
  26.1 1.3 collective-permute-start.5
  27.4 1.3 collective-permute-start.4
  28.7 0.1 maximum_maximum_fusion.1
  28.8 0.4 fusion.9
  29.2 0.0 collective-permute-done.5
  29.2 3.5 %collective-permute-done.4 = bf16[64,10,10,1]{0,3,2,1:T(2,128)(2,1)S(1)} collective-permute-done((bf16[64,10,10,1]{0,3,2,1:T(2,128)(2,1)S(1)}, bf16[64,10,10,1]{0,3,2,1:T(2,128)(2,1)S(1)}, u32[]{:S(2)}, u32[]{:S(2)}) %collective-permute-start.4) | collective-permute-done | bytes 12832 | tf_op jit(solution)/shard_map/ppermute | solution.py:19
  32.7 0.4 maximum_maximum_fusion
  33.1 2.3 %fusion.7 = (bf16[64,8,8,16]{0,3,2,1:T(8,128)(2,1)}, bf16[64,8,8,16]{0,3,2,1:T(8,128)(2,1)}, bf16[64,8,8,16]{0,3,2,1:T(8,128)(2,1)}, bf16[64,8,8,16]{0,3,2,1:T(8...) fusion(bf16[64,10,10,17]{0,3,2,1:T(8,128)(2,1)S(1)} %get-tuple-, ...), kind=kLoop, calls=%fused_computation.27 | loop fusion | bytes 4718592 | tf_op jit(solution)/shard_map/slice | solution.py:41
  35.3 2.6 %concatenate.65 = bf16[576,1024]{0,1:T(8,128)(2,1)S(1)} concatenate(bf16[64,1024]{0,1:T(8,128)(2,1)} %bitcast.66, bf16[64,1024]{0,1:T(8,128)(2,1)S(1)} %bitcast.50, bf16[64,1024]{0,1:T(8,128)(2,1)} %bitcast.65, bf16[64,1024]{0,1:T(8,128)(2,1)} %bitcast.67, bf16[64,1024]{0,1:T(8,128)(2,1)S(1)} %bitcast.41, bf16[64,1024]{0,1:T(8,128)(2,1)} %bitcast.64, bf16[64,1024]{0,1:T(8,128)(2,1)} %bitcast.68, ...), dimensions={0} | concatenate | bytes 2359296 | tf_op jit(solution)/shard_map/concatenate | solution.py:48
  38.0 2.1 %fusion.4 = f32[1024,64]{0,1:T(8,128)} fusion(bf16[576,1024]{0,1:T(8,128)(2,1)S(1)} %concatenate.65, bf16[64,1728]{1,0:T(8,128)(2,1)} %param.9), kind=kOutput, calls=%fused_computation.15 | convolution fusion | flops 75497472 | bytes 1523712 | tf_op jit(solution)/shard_map/dot_general | solution.py:51
  40.1 0.0 copy-start.5
  40.1 0.0 copy-start.6
  40.1 0.0 copy-start.7
  40.1 1.0 fusion.13
  41.1 0.0 copy-done.5
  41.1 0.0 copy-done.6
  41.1 0.1 copy-done.7
  41.2 2.5 %concatenate.64 = bf16[576,1024]{0,1:T(8,128)(2,1)S(1)} concatenate(bf16[64,1024]{0,1:T(8,128)(2,1)} %bitcast.60, bf16[64,1024]{0,1:T(8,128)(2,1)S(1)} %bitcast.48, bf16[64,1024]{0,1:T(8,128)(2,1)S(1)} %bitcast.59, bf16[64,1024]{0,1:T(8,128)(2,1)} %bitcast.61, bf16[64,1024]{0,1:T(8,128)(2,1)} %bitcast.70, bf16[64,1024]{0,1:T(8,128)(2,1)S(1)} %bitcast.58, ...), dimensions={0} | concatenate | bytes 2359296 | tf_op jit(solution)/shard_map/concatenate | solution.py:48
  43.8 0.0 copy-start.9
  43.8 1.0 fusion.12
  44.8 0.0 copy-done.9
  44.8 0.0 copy-start
  44.8 0.0 copy-start.1
  44.8 0.0 copy-start.2
  44.8 0.0 copy-start.3
  44.8 0.0 copy-start.4
  44.8 2.2 %convolution_add_fusion.1 = f32[1024,64]{0,1:T(8,128)} fusion(f32[1024,64]{0,1:T(8,128)S(1)} %copy-done.9, bf16[576,1024]{0,1:T(8,128)(2,1)S(1)} %concatenate.64, bf16[64,1728]{1,0:T(8,128)(2,1)} %param.9), kind=kOutput, calls=%fused_computation.2 | convolution fusion | flops 75563008 | bytes 1785856 | tf_op jit(solution)/shard_map/dot_general | solution.py:51
  47.0 0.0 copy-done
  47.0 0.0 copy-done.1
  47.0 0.0 copy-done.2
  47.0 0.0 copy-done.3
  47.0 0.0 copy-done.4
  47.0 2.4 %concatenate.67 = bf16[576,1024]{0,1:T(8,128)(2,1)S(1)} concatenate(bf16[64,1024]{0,1:T(8,128)(2,1)S(1)} %bitcast.54, bf16[64,1024]{0,1:T(8,128)(2,1)S(1)} %bitcast.46, bf16[64,1024]{0,1:T(8,128)(2,1)S(1)} %bitcast.53, bf16[64,1024]{0,1:T(8,128)(2,1)S(1)} %bitcast.55, bf16[64,1024]{0,1:T(8,128)(2,1)} %bitcast.69, bf16[64,1024]{0,1:T(8,128)(2,1)S(1)} %bitcast.52, ...), dimensions={0} | concatenate | bytes 2359296 | tf_op jit(solution)/shard_map/concatenate | solution.py:48
  49.5 0.0 copy-start.10
  49.5 0.0 copy-start.11
  49.5 0.0 copy-start.8
  49.5 0.3 fusion.14
  49.9 0.5 copy-done.10
  50.4 0.1 copy-done.11
  50.5 0.9 concatenate.68
  51.3 0.0 all-reduce.2.cloned.1.call-update
  51.4 0.0 copy-done.8
  51.4 1.4 fusion.2
  52.8 0.8 copy.8
  53.6 128.2 %all-reduce.2.cloned.1.call-done = f32[64,1728]{1,0:T(8,128)} async-done(((f32[64,1728]{1,0:T(8,128)}), f32[64,1728]{1,0:T(8,128)}) %all-reduce.2.cloned.1.call-update) | async-done | bytes 442384 | tf_op jit(solution)/shard_map/psum | solution.py:57
  181.8 1.8 broadcast_multiply_fusion
  (2 shorter events, 0.0 us)
Async XLA Ops:
  7.2 174.6 %all-reduce.2.cloned.1.call-start = ((), (), s32[]{:S(2)}) async-start(), calls=%async_computation | async-start | bytes 917504 | tf_op jit(solution)/shard_map/psum | solution.py:57
  10.0 7.0 %collective-permute-start.1 = (bf16[64,1,8,16]{0,3,2,1:T(8,128)(2,1)S(1)}, bf16[64,1,8,16]{0,3,2,1:T(8,128)(2,1)S(1)}, u32[]{:S(2)}, u32[]{:S(2)}) collective-permute-start(bf16[64,1,8,16]{0,3,2,1:T(8,128)(2,1)S(1)} %get-tuple-element.39), channel_id=1, source_target_pairs={{8,0},{16,8},{24,16},{9,1},{17,9},{25,17},{10,2},{18,10},{26,18},{... | collective-permute-start | bytes 49160 | tf_op jit(solution)/shard_map/ppermute | solution.py:19
  11.3 7.1 %collective-permute-start = (bf16[64,1,8,16]{0,3,2,1:T(8,128)(2,1)S(1)}, bf16[64,1,8,16]{0,3,2,1:T(8,128)(2,1)S(1)}, u32[]{:S(2)}, u32[]{:S(2)}) collective-permute-start(bf16[64,1,8,16]{0,3,2,1:T(8,128)(2,1)S(1)} %get-tuple-element.38), channel_id=1, source_target_pairs={{0,8},{8,16},{16,24},{1,9},{9,17},{17,25},{2,10},{10,18},{18,26},{... | collective-permute-start | bytes 49160 | tf_op jit(solution)/shard_map/ppermute | solution.py:18
  18.5 6.7 %collective-permute-start.3 = (bf16[64,10,1,16]{0,3,2,1:T(8,128)(2,1)S(1)}, bf16[64,10,1,16]{0,3,2,1:T(8,128)(2,1)S(1)}, u32[]{:S(2)}, u32[]{:S(2)}) collective-permute-start(bf16[64,10,1,16]{0,3,2,1:T(8,128)(2,1)S(1)} %get-tuple-element.35), channel_id=1, source_target_pairs={{4,0},{5,1},{6,2},{7,3},{12,8},{13,9},{14,10},{15,11},{20,16},{21,... | collective-permute-start | bytes 61448 | tf_op jit(solution)/shard_map/ppermute | solution.py:19
  19.8 6.2 %collective-permute-start.2 = (bf16[64,10,1,16]{0,3,2,1:T(8,128)(2,1)S(1)}, bf16[64,10,1,16]{0,3,2,1:T(8,128)(2,1)S(1)}, u32[]{:S(2)}, u32[]{:S(2)}) collective-permute-start(bf16[64,10,1,16]{0,3,2,1:T(8,128)(2,1)S(1)} %get-tuple-element.34), channel_id=1, source_target_pairs={{0,4},{1,5},{2,6},{3,7},{8,12},{9,13},{10,14},{11,15},{16,20},{17,... | collective-permute-start | bytes 61448 | tf_op jit(solution)/shard_map/ppermute | solution.py:18
  26.1 3.1 %collective-permute-start.5 = (bf16[64,10,10,1]{0,3,2,1:T(2,128)(2,1)S(1)}, bf16[64,10,10,1]{0,3,2,1:T(2,128)(2,1)S(1)}, u32[]{:S(2)}, u32[]{:S(2)}) collective-permute-start(bf16[64,10,10,1]{0,3,2,1:T(2,128)(2,1)S(1)} %get-tuple-element.24), channel_id=1, source_target_pairs={{0,1},{1,2},{2,3},{4,5},{5,6},{6,7},{8,9},{9,10},{10,11},{12,13},{... | collective-permute-start | bytes 38408 | tf_op jit(solution)/shard_map/ppermute | solution.py:18
  27.4 5.3 %collective-permute-start.4 = (bf16[64,10,10,1]{0,3,2,1:T(2,128)(2,1)S(1)}, bf16[64,10,10,1]{0,3,2,1:T(2,128)(2,1)S(1)}, u32[]{:S(2)}, u32[]{:S(2)}) collective-permute-start(bf16[64,10,10,1]{0,3,2,1:T(2,128)(2,1)S(1)} %get-tuple-element.25), channel_id=1, source_target_pairs={{1,0},{2,1},{3,2},{5,4},{6,5},{7,6},{9,8},{10,9},{11,10},{13,12},{... | collective-permute-start | bytes 38408 | tf_op jit(solution)/shard_map/ppermute | solution.py:19
  40.1 1.0 copy-start.5
  40.1 1.0 copy-start.6
  40.1 1.1 copy-start.7
  43.8 1.0 copy-start.9
  44.8 2.3 %copy-start = (bf16[64,8,8,16]{0,3,2,1:T(8,128)(2,1)S(1)}, bf16[64,8,8,16]{0,3,2,1:T(8,128)(2,1)}, u32[]{:S(2)}) copy-start(bf16[64,8,8,16]{0,3,2,1:T(8,128)(2,1)} %get-tuple-element.4) | copy-start | bytes 393220
  44.8 2.3 %copy-start.1 = (bf16[64,8,8,16]{0,3,2,1:T(8,128)(2,1)S(1)}, bf16[64,8,8,16]{0,3,2,1:T(8,128)(2,1)}, u32[]{:S(2)}) copy-start(bf16[64,8,8,16]{0,3,2,1:T(8,128)(2,1)} %get-tuple-element.5) | copy-start | bytes 393220
  44.8 2.3 %copy-start.2 = (bf16[64,8,8,16]{0,3,2,1:T(8,128)(2,1)S(1)}, bf16[64,8,8,16]{0,3,2,1:T(8,128)(2,1)}, u32[]{:S(2)}) copy-start(bf16[64,8,8,16]{0,3,2,1:T(8,128)(2,1)} %get-tuple-element.6) | copy-start | bytes 393220
  44.8 2.3 %copy-start.3 = (bf16[64,8,8,16]{0,3,2,1:T(8,128)(2,1)S(1)}, bf16[64,8,8,16]{0,3,2,1:T(8,128)(2,1)}, u32[]{:S(2)}) copy-start(bf16[64,8,8,16]{0,3,2,1:T(8,128)(2,1)} %get-tuple-element.48) | copy-start | bytes 393220
  44.8 2.3 %copy-start.4 = (bf16[64,8,8,16]{0,3,2,1:T(8,128)(2,1)S(1)}, bf16[64,8,8,16]{0,3,2,1:T(8,128)(2,1)}, u32[]{:S(2)}) copy-start(bf16[64,8,8,16]{0,3,2,1:T(8,128)(2,1)} %get-tuple-element.49) | copy-start | bytes 393220
  49.5 0.9 copy-start.10
  49.5 1.0 copy-start.11
  49.5 1.9 copy-start.8
Sparse Core Ops, SparseCore 0:
  51.5 130.2 all-reduce.1
where the time goes:
time: 192 us; the launch traced here: 190 us
  waiting for transfers between devices  134 us (70%)
  starting transfers between devices  15.3 us (8%)
  between operations  14.3 us (7%)
  local copies, waits for them, and re-layouts  13.6 us (7%)
  matrix products  8.12 us (4%)
  other arithmetic  5.29 us (3%)
    psum x1, waiting for transfers between devices, local(): grad_weight = lax.psum(grad_weight, ('gx', 'gy', 'gz'))  128 us
    ppermute x3, starting transfers between devices, extended(): before = lax.ppermute(last, axis, up)  11.4 us
    concatenate x3, local copies, waits for them, and re-layouts, local(): columns = jnp.concatenate(pieces, axis=0)  7.56 us
    dot_general x3, matrix products, local(): jnp.dot(kernel_plane, columns, preferred_element_type=jnp.float32)  5.78 us
    ppermute x3, starting transfers between devices, extended(): after = lax.ppermute(initial, axis, down)  3.88 us
  transfers between devices with their start and end apart: 7, of which 4 were waited for; matrix products, arithmetic and copies ran while one was open for 2% of the time, Pallas kernels for 0%

commit v1 on v0

v1 whole, which is shorter than its diff:
```python
import functools
import math

import jax
import jax.numpy as jnp
from jax import lax
from jax.experimental import pallas as pl
from jax.experimental.pallas import tpu as pltpu
from jax.sharding import PartitionSpec as P

BRICK = 8
MESH = pl.DeviceIdType.MESH
F32, BF16 = jnp.float32, jnp.bfloat16


def ceil_div(a, b):
    return -(-a // b)


def plan(n_gx, n_gy, n_gz, chans):
    cores = 2 if n_gz % 2 == 0 else 1
    plane = n_gy * (n_gz // cores)
    tiles = 27 * chans * chans // 1024
    part2 = ceil_div(ceil_div(tiles, cores), plane)
    part1 = part2 * plane
    part3 = ceil_div(part2, n_gx)
    return cores, plane, tiles, part1, part2, part3


def iota(shape, dim):
    return lax.broadcasted_iota(jnp.int32, shape, dim)


def kernel(
    sizes, scale, g_ref, f_ref, b_ref, v_ref, w_ref, gi_ref, gw_ref,
    pad, cols, mask, faces, rims, terms, in1, in2, sum2, in3, out3, full,
    halo_send, halo_recv, core_send, core_recv, plane_send, plane_recv, line_send, line_recv,
):
    n_gx, n_gy, n_gz = sizes
    sx, sy, sz, chans = g_ref.shape
    nxy, count = sx * sy, sx * sy * sz
    cores, plane, tiles, part1, part2, part3 = plan(n_gx, n_gy, n_gz, chans)
    gx, gy, gz = lax.axis_index("gx"), lax.axis_index("gy"), lax.axis_index("gz")
    core, xh = lax.rem(gz, cores), gz // cores
    wide = n_gz // cores
    spot = gy * wide + xh

    def plane_peer(step):
        other = lax.rem(spot + step, plane)
        return (gx, other // wide, lax.rem(other, wide) * cores + core)

    def line_peer(step):
        return (lax.rem(gx + step, n_gx), gy, gz)

    core_peer = (gx, gy, xh * cores + (cores - 1 - core))
    partners = [plane_peer(s) for s in range(1, plane)] + [line_peer(s) for s in range(1, n_gx)]
    if cores == 2:
        partners.append(core_peer)
    if n_gz > cores:
        partners.append((gx, gy, lax.rem(gz + n_gz + 2 * core - 1, n_gz)))
    barrier = pltpu.get_barrier_semaphore()
    for partner in partners:
        pl.semaphore_signal(barrier, inc=1, device_id=partner, device_id_type=MESH)

    bricks = jnp.zeros((sx, sy, sz), jnp.int32)
    at = [iota((sx, sy, sz), d) // BRICK for d in range(3)]
    for i in range(b_ref.shape[0]):
        for j in range(b_ref.shape[1]):
            for l in range(b_ref.shape[2]):
                here = (at[0] == i) & (at[1] == j) & (at[2] == l)
                bricks = jnp.where(here, b_ref[i, j, l], bricks)
    active = jnp.where(bricks * v_ref[...] > 0, 1.0, 0.0).reshape(nxy, sz).astype(BF16)
    own = jnp.where(iota((count, nxy), 0) // sz == iota((count, nxy), 1), 1.0, 0.0).astype(BF16)
    spread = jnp.dot(own, active, preferred_element_type=F32)
    level = lax.rem(iota((count, sz), 0), sz) == iota((count, sz), 1)
    spread = jnp.where(level, spread, 0.0).astype(BF16)
    lit = jnp.dot(spread, jnp.ones((sz, chans), BF16), preferred_element_type=F32)
    mask[...] = lit
    lit = lit.astype(BF16)
    grad = g_ref[...].reshape(count, chans) * lit

    row, col = iota((2 * nxy, count), 0), iota((2 * nxy, count), 1)
    pick = jnp.where(row < nxy, row * sz, (row - nxy) * sz + sz - 1) == col
    pick = jnp.where(pick, 1.0, 0.0).astype(BF16)
    ends = jnp.dot(pick, grad, preferred_element_type=F32)
    zeros = jnp.zeros((2 * nxy, chans), F32)
    faces[...] = jnp.concatenate([zeros, ends], axis=1).astype(BF16)

    pl.semaphore_wait(barrier, len(partners))

    def swap(base, index, length, device, low_src, high_src, low_dst, high_dst):
        def down():
            return pltpu.make_async_remote_copy(
                src_ref=low_src, dst_ref=high_dst, send_sem=halo_send.at[base],
                recv_sem=halo_recv.at[base], device_id=device(lax.rem(index + length - 1, length)),
                device_id_type=MESH,
            )

        def up():
            return pltpu.make_async_remote_copy(
                src_ref=high_src, dst_ref=low_dst, send_sem=halo_send.at[base + 1],
                recv_sem=halo_recv.at[base + 1], device_id=device(lax.rem(index + 1, length)),
                device_id_type=MESH,
            )

        if length > 1:
            @pl.when(index > 0)
            def _():
                down().start()

            @pl.when(index < length - 1)
            def _():
                up().start()

        def finish():
            @pl.when(index == 0)
            def _():
                low_dst[...] = jnp.zeros(low_dst.shape, low_dst.dtype)

            @pl.when(index == length - 1)
            def _():
                high_dst[...] = jnp.zeros(high_dst.shape, high_dst.dtype)

            if length > 1:
                @pl.when(index > 0)
                def _():
                    up().wait_recv()
                    down().wait_send()

                @pl.when(index < length - 1)
                def _():
                    down().wait_recv()
                    up().wait_send()

        return finish

    def columns(tile):
        lead = tile.shape[:-2]
        rows = math.prod(tile.shape[:-1])
        wide_tile = tile.reshape(rows, 2 * chans).astype(F32)
        after = pltpu.roll(wide_tile, rows - 1, 0)
        before = pltpu.roll(wide_tile, 1, 0)
        other = pltpu.roll(wide_tile, chans, 1)
        z, lane = lax.rem(iota(wide_tile.shape, 0), sz), iota(wide_tile.shape, 1)
        first = jnp.where((lane < chans) & (z != sz - 1), after, other)
        second = jnp.where(z == 0, other, before)
        both = jnp.concatenate([first, second], axis=1).astype(BF16)
        return both.reshape(*lead, sz, 4 * chans)

    finish = swap(
        0, gz, n_gz, lambda i: (gx, gy, i),
        faces.at[pl.ds(0, nxy)], faces.at[pl.ds(nxy, nxy)],
        rims.at[pl.ds(0, nxy)], rims.at[pl.ds(nxy, nxy)],
    )
    feat = (f_ref[...].reshape(count, chans) * lit).astype(F32).T.astype(BF16)
    finish()
    row, col = iota((count, 2 * nxy), 0), iota((count, 2 * nxy), 1)
    place = jnp.where(col < nxy, col * sz, (col - nxy) * sz + sz - 1) == row
    place = jnp.where(place, 1.0, 0.0).astype(BF16)
    rim = jnp.dot(place, rims[...], preferred_element_type=F32)
    body = jnp.concatenate([grad.astype(F32), jnp.zeros((count, chans), F32)], axis=1) + rim
    pad[1 : sx + 1, 1 : sy + 1] = body.astype(BF16).reshape(sx, sy, sz, 2 * chans)

    inner = pl.ds(1, sy)
    finish = swap(
        2, gx, n_gx, lambda i: (i, gy, gz),
        pad.at[1, inner], pad.at[sx, inner], pad.at[0, inner], pad.at[sx + 1, inner],
    )
    cols[1 : sx + 1, 1 : sy + 1] = columns(pad[1 : sx + 1, 1 : sy + 1])
    finish()
    finish = swap(
        4, gy, n_gy, lambda i: (gx, i, gz),
        pad.at[:, 1], pad.at[:, sy], pad.at[:, 0], pad.at[:, sy + 1],
    )
    cols[0, 1 : sy + 1] = columns(pad[0, 1 : sy + 1])
    cols[sx + 1, 1 : sy + 1] = columns(pad[sx + 1, 1 : sy + 1])

    half = chans // 2
    per = half // 8

    def shifted(a, b):
        return cols[1 - a : 1 - a + sx, 1 - b : 1 - b + sy].reshape(count, 4 * chans)

    def weight_term(a, b):
        got = jnp.dot(feat, shifted(a, b), preferred_element_type=F32)
        low = iota((half, 2 * chans), 1) < chans
        for e in range(3):
            tile = e // 2
            top = got[:half, tile * 2 * chans : (tile + 1) * 2 * chans]
            end = got[half:, tile * 2 * chans : (tile + 1) * 2 * chans]
            if e % 2 == 0:
                both = jnp.where(low, top, pltpu.roll(end, chans, 1))
            else:
                both = jnp.where(low, pltpu.roll(top, chans, 1), end)
            k = 9 * (a + 1) + 3 * (b + 1) + e
            terms[k * per : (k + 1) * per] = both.reshape(per, 8, 2 * chans)

    for a in (-1, 0, 1):
        weight_term(a, 0)
    if cores * part1 > tiles:
        terms[tiles:] = jnp.zeros((cores * part1 - tiles, 8, 2 * chans), F32)
    finish()
    cols[:, 0] = columns(pad[:, 0])
    cols[:, sy + 1] = columns(pad[:, sy + 1])
    for a in (-1, 0, 1):
        weight_term(a, -1)
        weight_term(a, 1)

    def send(src, dst, send_sem, recv_sem, device):
        copy = pltpu.make_async_remote_copy(
            src_ref=src, dst_ref=dst, send_sem=send_sem, recv_sem=recv_sem,
            device_id=device, device_id_type=MESH,
        )
        copy.start()
        return copy

    flights = []
    base1 = core * part1
    if cores == 2:
        flights = [send(terms.at[pl.ds((1 - core) * part1, part1)], in1, core_send.at[0],
                        core_recv.at[0], core_peer)]

    def input_rows(x):
        wide_cols, kernels = [], []
        for a in (-1, 0, 1):
            for b in (-1, 0, 1):
                rows = cols[x + 1 - a, 1 - b : 1 - b + sy].reshape(sy * sz, 4 * chans)
                k = 9 * (a + 1) + 3 * (b + 1)
                wide_cols.append(rows[:, : 3 * chans])
                kernels.append(w_ref[:, k * chans : (k + 3) * chans])
        total = jnp.zeros((sy * sz, chans), F32)
        for rows, kern in zip(wide_cols, kernels):
            total = total + lax.dot_general(
                rows, kern, (((1,), (1,)), ((), ())), preferred_element_type=F32
            )
        keep = mask[x * sy * sz : (x + 1) * sy * sz] > 0
        gi_ref[x] = jnp.where(keep, total, 0.0).astype(BF16).reshape(sy, sz, chans)

    for x in range(sx // 2):
        input_rows(x)
    mine = pl.ds(base1, part1)
    for copy in flights:
        copy.wait()
        terms[mine] = terms[mine] + in1[...]
    flights = []
    for step in range(1, plane):
        other = lax.rem(spot + step, plane)
        flights.append(send(
            terms.at[pl.ds(base1 + other * part2, part2)], in2.at[step - 1],
            plane_send.at[step - 1], plane_recv.at[step - 1], plane_peer(step),
        ))
    for x in range(sx // 2, sx):
        input_rows(x)
    acc = terms[pl.ds(base1 + spot * part2, part2)]
    for step, copy in enumerate(flights):
        copy.wait()
        acc = acc + in2[step]
    sum2[:part2] = acc
    if n_gx * part3 > part2:
        sum2[part2:] = jnp.zeros((n_gx * part3 - part2, 8, 2 * chans), F32)
    flights = []
    for step in range(1, n_gx):
        other = lax.rem(gx + step, n_gx)
        flights.append(send(
            sum2.at[pl.ds(other * part3, part3)], in3.at[step - 1],
            line_send.at[step - 1], line_recv.at[step - 1], line_peer(step),
        ))
    acc = sum2[pl.ds(gx * part3, part3)]
    for step, copy in enumerate(flights):
        copy.wait()
        acc = acc + in3[step]

    out3[pl.ds(gx * part3, part3)] = acc * scale
    flights = []
    for step in range(1, n_gx):
        here = out3.at[pl.ds(gx * part3, part3)]
        slot = n_gx - 1 + step - 1
        flights.append(send(here, here, line_send.at[slot], line_recv.at[slot], line_peer(step)))
    for copy in flights:
        copy.wait()
    flights = []
    here = pl.ds(base1 + spot * part2, part2)
    for step in range(1, plane):
        slot = plane - 1 + step - 1
        flights.append(send(
            out3.at[pl.ds(0, part2)], full.at[here],
            plane_send.at[slot], plane_recv.at[slot], plane_peer(step),
        ))
    full[here] = out3[:part2]
    for copy in flights:
        copy.wait()
    if cores == 2:
        send(full.at[mine], full.at[mine], core_send.at[1], core_recv.at[1], core_peer).wait()

    low = iota((half, 2 * chans), 1) < chans
    for k in range(0, 27, 2):
        one = full[k * per : (k + 1) * per].reshape(half, 2 * chans)
        if k == 26:
            gw_ref[:half, k * chans :] = one[:, :chans]
            gw_ref[half:, k * chans :] = pltpu.roll(one, chans, 1)[:, :chans]
            continue
        two = full[(k + 1) * per : (k + 2) * per].reshape(half, 2 * chans)
        at_k = slice(k * chans, (k + 2) * chans)
        gw_ref[:half, at_k] = jnp.where(low, one, pltpu.roll(two, chans, 1))
        gw_ref[half:, at_k] = jnp.where(low, pltpu.roll(one, chans, 1), two)


def local(sizes, grad_out, features, brick_mask, voxel_mask, weight):
    chans, sx, sy, sz = grad_out.shape
    n_gx, n_gy, n_gz = sizes
    cores, plane, tiles, part1, part2, part3 = plan(n_gx, n_gy, n_gz, chans)
    scale = 1.0 / math.sqrt(sx * sy * sz * n_gx * n_gy * n_gz)
    vmem = pl.BlockSpec(memory_space=pltpu.VMEM)
    dma = lambda n: pltpu.SemaphoreType.DMA((max(n, 1),))
    tile = (8, 2 * chans)
    grad_input, grad_weight = pl.pallas_call(
        functools.partial(kernel, sizes, scale),
        out_shape=(
            jax.ShapeDtypeStruct((sx, sy, sz, chans), BF16),
            jax.ShapeDtypeStruct((chans, 27 * chans), F32),
        ),
        in_specs=[vmem, vmem, pl.BlockSpec(memory_space=pltpu.SMEM), vmem, vmem],
        out_specs=(vmem, vmem),
        scratch_shapes=[
            pltpu.VMEM((sx + 2, sy + 2, sz, 2 * chans), BF16),
            pltpu.VMEM((sx + 2, sy + 2, sz, 4 * chans), BF16),
            pltpu.VMEM((sx * sy * sz, chans), F32),
            pltpu.VMEM((2 * sx * sy, 2 * chans), BF16),
            pltpu.VMEM((2 * sx * sy, 2 * chans), BF16),
            pltpu.VMEM((cores * part1, *tile), F32),
            pltpu.VMEM((part1, *tile), F32),
            pltpu.VMEM((max(plane - 1, 1), part2, *tile), F32),
            pltpu.VMEM((n_gx * part3, *tile), F32),
            pltpu.VMEM((max(n_gx - 1, 1), part3, *tile), F32),
            pltpu.VMEM((n_gx * part3, *tile), F32),
            pltpu.VMEM((cores * part1, *tile), F32),
            dma(6), dma(6), dma(2), dma(2),
            dma(2 * (plane - 1)), dma(2 * (plane - 1)),
            dma(2 * (n_gx - 1)), dma(2 * (n_gx - 1)),
        ],
        compiler_params=pltpu.CompilerParams(
            collective_id=0, has_side_effects=True, vmem_limit_bytes=40 * 1024 * 1024
        ),
    )(
        jnp.transpose(grad_out, (1, 2, 3, 0)),
        jnp.transpose(features, (1, 2, 3, 0)),
        brick_mask,
        voxel_mask,
        weight,
    )
    return jnp.transpose(grad_input, (3, 0, 1, 2)), grad_weight


def solution(mesh):
    sizes = tuple(mesh.shape[name] for name in ("gx", "gy", "gz"))
    return jax.shard_map(
        functools.partial(local, sizes),
        mesh=mesh,
        in_specs=(
            P(None, "gx", "gy", "gz"),
            P(None, "gx", "gy", "gz"),
            P("gx", "gy", "gz"),
            P("gx", "gy", "gz"),
            P(),
        ),
        out_specs=(P(None, "gx", "gy", "gz"), P()),
        check_vma=False,
    )
```

time: 192 us -> 40 us (0.21)
  waiting for transfers between devices: 134 us -> 0 us
  Pallas kernels: 0 us -> 33.4 us
  starting transfers between devices: 15.3 us -> 0 us
  between operations: 14.3 us -> 0.65 us
  matrix products: 8.12 us -> 0 us
  local copies, waits for them, and re-layouts: 13.6 us -> 5.71 us
  other arithmetic: 5.29 us -> 0 us
    psum x1 -> x0, waiting for transfers between devices: 128 us -> none  [local(): grad_weight = lax.psum(grad_weight, ('gx', 'gy', 'gz'))]
    pallas_call x0 -> x1, Pallas kernels: none -> 33.4 us  [local(): pl.pallas_call(functools.partial(kernel, sizes, scale), out_shape=(jax.Sh...]
    ppermute x6 -> x0, starting transfers between devices: 15.3 us -> none  [the longest x3 11.4 us: extended(): before = lax.ppermute(last, axis, up)]
    concatenate x4 -> x0, local copies, waits for them, and re-layouts: 8.44 us -> none  [the longest x3 7.56 us: local(): columns = jnp.concatenate(pieces, axis=0)]
    dot_general x6 -> x0, matrix products: 8.12 us -> none  [the longest x3 5.78 us: local(): jnp.dot(kernel_plane, columns, preferred_element_type=jnp.float32)]
    ppermute x6 -> x0, waiting for transfers between devices: 5.76 us -> none  [the longest x3 3.49 us: extended(): after = lax.ppermute(initial, axis, down)]
    unnamed x24 -> x12, local copies, waits for them, and re-layouts: 0.75 us -> 5.71 us
    slice x3 -> x0, local copies, waits for them, and re-layouts: 2.64 us -> none  [the longest x2 2.64 us: local(): padded[:, 1 - shift_x:1 - shift_x + size_x, 1 - shift_y:1 - shift_y + siz...]
  transfers between devices with their start and end apart: 7 -> 0, of which waited for: 4 -> 0; matrix products, arithmetic and copies ran while one was open for 2% -> 0% of each run, Pallas kernels for 0% -> 0%
where the time goes in v1:
time: 40 us; the launch traced here: 39.8 us
  Pallas kernels  33.4 us (84%)
  local copies, waits for them, and re-layouts  5.71 us (14%)
  between operations  0.65 us (2%)
    pallas_call x1, Pallas kernels, local(): pl.pallas_call(functools.partial(kernel, sizes, scale), out_shape=(jax.Sh...  33.4 us
    unnamed x12, local copies, waits for them, and re-layouts  5.71 us

profile of v1, /device:TPU:0, one launch (start us, length us, event | category | flops | bytes accessed | tf_op | source)
XLA Modules:
  0.0 39.8 jit_solution(6485365245729675185)
XLA Ops:
  0.6 0.0 copy-start.4
  0.6 0.6 %copy-done.4 = s32[1,1,2]{2,1,0:T(1,128)S(1)} copy-done((s32[1,1,2]{2,1,0:T(1,128)S(1)}, s32[1,1,2]{2,1,0:T(1,128)}, u32[]{:S(2)}) %copy-start.4) | copy-done | bytes 32
  1.3 0.0 copy-start
  1.3 0.9 %copy-done = bf16[64,8,8,16]{0,3,2,1:T(8,128)(2,1)S(1)} copy-done((bf16[64,8,8,16]{0,3,2,1:T(8,128)(2,1)S(1)}, bf16[64,8,8,16]{0,3,2,1:T(8,128)(2,1)}, u32[]{:S(2)}) %copy-start) | copy-done | bytes 131096
  2.2 0.0 copy-start.1
  2.2 0.9 %copy-done.1 = bf16[64,8,8,16]{0,3,2,1:T(8,128)(2,1)S(1)} copy-done((bf16[64,8,8,16]{0,3,2,1:T(8,128)(2,1)S(1)}, bf16[64,8,8,16]{0,3,2,1:T(8,128)(2,1)}, u32[]{:S(2)}) %copy-start.1) | copy-done | bytes 131096
  3.2 0.0 copy-start.2
  3.2 0.9 %copy-done.2 = bf16[64,1728]{1,0:T(8,128)(2,1)S(1)} copy-done((bf16[64,1728]{1,0:T(8,128)(2,1)S(1)}, bf16[64,1728]{1,0:T(8,128)(2,1)}, u32[]{:S(2)}) %copy-start.2) | copy-done | bytes 221208
  4.1 0.0 copy-start.3
  4.1 0.8 %copy-done.3 = s32[8,8,16]{2,1,0:T(8,128)S(1)} copy-done((s32[8,8,16]{2,1,0:T(8,128)S(1)}, s32[8,8,16]{2,1,0:T(8,128)}, u32[]{:S(2)}) %copy-start.3) | copy-done | bytes 4120
  4.9 33.4 %shard_map.68 = (bf16[8,8,16,64]{3,2,1,0:T(8,128)(2,1)S(1)}, f32[64,1728]{1,0:T(8,128)S(1)}) custom-call(bf16[8,8,16,64]{3,2,1,0:T(8,128)(2,1)S(1)} %bitcast.4, bf16[8,8,16,64]{3,2,1,0:T(8,128)(2,1)S(1)} %bitcast.5, s32[1,1,2]{2,1,0:T(1,128)S(1)} %copy-done.4, s32[8,8,16]{2,1,0:T(8,128)S(1)} %copy-done.3, bf16[64,1728]{1,0:T(8,128)(2,1)S(1)} %copy-done.2), custom_call_target="tpu_custom_call" | custom-call | tf_op jit(solution)/shard_map/pallas_call | solution.py:316
  38.3 0.7 %copy.9 = bf16[64,8,8,16]{0,3,2,1:T(8,128)(2,1)} copy(bf16[64,8,8,16]{0,3,2,1:T(8,128)(2,1)S(1)} %bitcast.3) | data formatting | bytes 262144
  39.0 0.8 %copy.10 = f32[64,1728]{1,0:T(8,128)} copy(f32[64,1728]{1,0:T(8,128)S(1)} %get-tuple-element.9) | data formatting | bytes 884736
Async XLA Ops:
  0.6 0.7 %copy-start.4 = (s32[1,1,2]{2,1,0:T(1,128)S(1)}, s32[1,1,2]{2,1,0:T(1,128)}, u32[]{:S(2)}) copy-start(s32[1,1,2]{2,1,0:T(1,128)} %b_ref.1) | copy-start | bytes 28
  1.3 0.9 %copy-start = (bf16[64,8,8,16]{0,3,2,1:T(8,128)(2,1)S(1)}, bf16[64,8,8,16]{0,3,2,1:T(8,128)(2,1)}, u32[]{:S(2)}) copy-start(bf16[64,8,8,16]{0,3,2,1:T(8,128)(2,1)} %param.5) | copy-start | bytes 393220
  2.2 0.9 %copy-start.1 = (bf16[64,8,8,16]{0,3,2,1:T(8,128)(2,1)S(1)}, bf16[64,8,8,16]{0,3,2,1:T(8,128)(2,1)}, u32[]{:S(2)}) copy-start(bf16[64,8,8,16]{0,3,2,1:T(8,128)(2,1)} %param.6) | copy-start | bytes 393220
  3.2 0.9 %copy-start.2 = (bf16[64,1728]{1,0:T(8,128)(2,1)S(1)}, bf16[64,1728]{1,0:T(8,128)(2,1)}, u32[]{:S(2)}) copy-start(bf16[64,1728]{1,0:T(8,128)(2,1)} %w_ref.1) | copy-start | bytes 663556
  4.1 0.8 %copy-start.3 = (s32[8,8,16]{2,1,0:T(8,128)S(1)}, s32[8,8,16]{2,1,0:T(8,128)}, u32[]{:S(2)}) copy-start(s32[8,8,16]{2,1,0:T(8,128)} %v_ref.1) | copy-start | bytes 12292

commit v2 on v1

v2 whole, which is shorter than its diff:
```python
import functools
import math

import jax
import jax.numpy as jnp
from jax import lax
from jax.experimental import pallas as pl
from jax.experimental.pallas import tpu as pltpu
from jax.sharding import PartitionSpec as P

BRICK = 8
MESH = pl.DeviceIdType.MESH
F32, BF16 = jnp.float32, jnp.bfloat16


def ceil_div(a, b):
    return -(-a // b)


def plan(sizes, chans):
    n_gx, n_gy, n_gz = sizes
    cores = 2 if n_gz % 2 == 0 else 1
    plane = n_gy * (n_gz // cores)
    tiles = 9 * chans * chans // 1024
    streams = []
    for count, order in ((tiles, (cores, n_gx, plane)), (2 * tiles, (cores, plane, n_gx))):
        stages, left = [], count
        for peers in order:
            left = ceil_div(left, peers)
            stages.append((peers, left))
        streams.append((count, stages))
    return cores, plane, streams


def div(x, n):
    return lax.shift_right_logical(x, n.bit_length() - 1) if n & (n - 1) == 0 else x // n


def mod(x, n):
    return x & (n - 1) if n & (n - 1) == 0 else lax.rem(x, n)


def iota(shape, dim):
    return lax.broadcasted_iota(jnp.int32, shape, dim)


def kernel(
    sizes, scale, g_hbm, f_hbm, b_hbm, v_hbm, w_hbm, gi_ref, gw_ref,
    g_ref, f_ref, b_ref, v_ref, w_ref, load_sem,
    pad, cols, mask, faces, rims, halo_send, halo_recv, *stream_refs,
):
    n_gx, n_gy, n_gz = sizes
    sx, sy, sz, chans = g_ref.shape
    nxy, count = sx * sy, sx * sy * sz
    cores, plane, streams = plan(sizes, chans)
    loads = [
        pltpu.make_async_copy(src, dst, load_sem.at[i])
        for i, (src, dst) in enumerate(
            [(b_hbm, b_ref), (v_hbm, v_ref), (g_hbm, g_ref), (f_hbm, f_ref), (w_hbm, w_ref)]
        )
    ]
    for load in loads:
        load.start()
    gx, gy, gz = lax.axis_index("gx"), lax.axis_index("gy"), lax.axis_index("gz")
    core, xh = lax.rem(gz, cores), gz // cores
    wide = n_gz // cores
    spot = gy * wide + xh

    def plane_peer(step):
        other = lax.rem(spot + step, plane)
        return (gx, other // wide, lax.rem(other, wide) * cores + core)

    def line_peer(step):
        return (lax.rem(gx + step, n_gx), gy, gz)

    def core_peer(step):
        return (gx, gy, xh * cores + lax.rem(core + step, cores))

    partners = [plane_peer(s) for s in range(1, plane)] + [line_peer(s) for s in range(1, n_gx)]
    if cores == 2:
        partners.append(core_peer(1))
    if n_gz > cores:
        partners.append((gx, gy, lax.rem(gz + n_gz + 2 * core - 1, n_gz)))
    barrier = pltpu.get_barrier_semaphore()
    for partner in partners:
        pl.semaphore_signal(barrier, inc=1, device_id=partner, device_id_type=MESH)

    bricks = jnp.zeros((sx, sy, sz), jnp.int32)
    loads[0].wait()
    loads[1].wait()
    at = [div(iota((sx, sy, sz), d), BRICK) for d in range(3)]
    for i in range(b_ref.shape[0]):
        for j in range(b_ref.shape[1]):
            for l in range(b_ref.shape[2]):
                here = (at[0] == i) & (at[1] == j) & (at[2] == l)
                bricks = jnp.where(here, b_ref[i, j, l], bricks)
    active = jnp.where(bricks * v_ref[...] > 0, 1.0, 0.0).reshape(nxy, sz).astype(BF16)
    own = jnp.where(div(iota((count, nxy), 0), sz) == iota((count, nxy), 1), 1.0, 0.0).astype(BF16)
    spread = jnp.dot(own, active, preferred_element_type=F32)
    level = mod(iota((count, sz), 0), sz) == iota((count, sz), 1)
    spread = jnp.where(level, spread, 0.0).astype(BF16)
    lit = jnp.dot(spread, jnp.ones((sz, chans), BF16), preferred_element_type=F32)
    mask[...] = lit
    lit = lit.astype(BF16)
    loads[2].wait()
    grad = g_ref[...].reshape(count, chans) * lit

    row, col = iota((2 * nxy, count), 0), iota((2 * nxy, count), 1)
    pick = jnp.where(row < nxy, row * sz, (row - nxy) * sz + sz - 1) == col
    pick = jnp.where(pick, 1.0, 0.0).astype(BF16)
    ends = jnp.dot(pick, grad, preferred_element_type=F32)
    zeros = jnp.zeros((2 * nxy, chans), F32)
    faces[...] = jnp.concatenate([zeros, ends], axis=1).astype(BF16)

    pl.semaphore_wait(barrier, len(partners))

    def swap(base, index, length, device, low_src, high_src, low_dst, high_dst):
        def down():
            return pltpu.make_async_remote_copy(
                src_ref=low_src, dst_ref=high_dst, send_sem=halo_send.at[base],
                recv_sem=halo_recv.at[base], device_id=device(lax.rem(index + length - 1, length)),
                device_id_type=MESH,
            )

        def up():
            return pltpu.make_async_remote_copy(
                src_ref=high_src, dst_ref=low_dst, send_sem=halo_send.at[base + 1],
                recv_sem=halo_recv.at[base + 1], device_id=device(lax.rem(index + 1, length)),
                device_id_type=MESH,
            )

        if length > 1:
            @pl.when(index > 0)
            def _():
                down().start()

            @pl.when(index < length - 1)
            def _():
                up().start()

        def finish():
            @pl.when(index == 0)
            def _():
                low_dst[...] = jnp.zeros(low_dst.shape, low_dst.dtype)

            @pl.when(index == length - 1)
            def _():
                high_dst[...] = jnp.zeros(high_dst.shape, high_dst.dtype)

            if length > 1:
                @pl.when(index > 0)
                def _():
                    up().wait_recv()
                    down().wait_send()

                @pl.when(index < length - 1)
                def _():
                    down().wait_recv()
                    up().wait_send()

        return finish

    def columns(tile):
        lead = tile.shape[:-2]
        rows = math.prod(tile.shape[:-1])
        wide_tile = tile.reshape(rows, 2 * chans).astype(F32)
        after = pltpu.roll(wide_tile, rows - 1, 0)
        before = pltpu.roll(wide_tile, 1, 0)
        other = pltpu.roll(wide_tile, chans, 1)
        z, lane = mod(iota(wide_tile.shape, 0), sz), iota(wide_tile.shape, 1)
        first = jnp.where((lane < chans) & (z != sz - 1), after, other)
        second = jnp.where(z == 0, other, before)
        both = jnp.concatenate([first, second], axis=1).astype(BF16)
        return both.reshape(*lead, sz, 4 * chans)

    finish = swap(
        0, gz, n_gz, lambda i: (gx, gy, i),
        faces.at[pl.ds(0, nxy)], faces.at[pl.ds(nxy, nxy)],
        rims.at[pl.ds(0, nxy)], rims.at[pl.ds(nxy, nxy)],
    )
    loads[3].wait()
    feat = (f_ref[...].reshape(count, chans) * lit).astype(F32).T.astype(BF16)
    finish()
    row, col = iota((count, 2 * nxy), 0), iota((count, 2 * nxy), 1)
    place = jnp.where(col < nxy, col * sz, (col - nxy) * sz + sz - 1) == row
    place = jnp.where(place, 1.0, 0.0).astype(BF16)
    rim = jnp.dot(place, rims[...], preferred_element_type=F32)
    body = jnp.concatenate([grad.astype(F32), jnp.zeros((count, chans), F32)], axis=1) + rim
    pad[1 : sx + 1, 1 : sy + 1] = body.astype(BF16).reshape(sx, sy, sz, 2 * chans)

    inner = pl.ds(1, sy)
    finish = swap(
        2, gx, n_gx, lambda i: (i, gy, gz),
        pad.at[1, inner], pad.at[sx, inner], pad.at[0, inner], pad.at[sx + 1, inner],
    )
    cols[1 : sx + 1, 1 : sy + 1] = columns(pad[1 : sx + 1, 1 : sy + 1])
    finish()
    finish = swap(
        4, gy, n_gy, lambda i: (gx, i, gz),
        pad.at[:, 1], pad.at[:, sy], pad.at[:, 0], pad.at[:, sy + 1],
    )
    cols[0, 1 : sy + 1] = columns(pad[0, 1 : sy + 1])
    cols[sx + 1, 1 : sy + 1] = columns(pad[sx + 1, 1 : sy + 1])

    half = chans // 2
    per = half // 8

    def shifted(a, b):
        return cols[1 - a : 1 - a + sx, 1 - b : 1 - b + sy].reshape(count, 4 * chans)

    def weight_term(a, b, terms, first):
        got = jnp.dot(feat, shifted(a, b), preferred_element_type=F32)
        low = iota((half, 2 * chans), 1) < chans
        for e in range(3):
            tile = e // 2
            top = got[:half, tile * 2 * chans : (tile + 1) * 2 * chans]
            end = got[half:, tile * 2 * chans : (tile + 1) * 2 * chans]
            if e % 2 == 0:
                both = jnp.where(low, top, pltpu.roll(end, chans, 1))
            else:
                both = jnp.where(low, pltpu.roll(top, chans, 1), end)
            at_tile = (first + e) * per
            terms[at_tile : at_tile + per] = both.reshape(per, 8, 2 * chans)

    class Stream:
        def __init__(self, which):
            self.tiles, self.stages = streams[which]
            refs = stream_refs[which * 15 : (which + 1) * 15]
            self.sums, self.ins, self.outs = refs[0:3], refs[3:6], refs[6:9]
            self.sends, self.recvs = refs[9:12], refs[12:15]
            across, along = (spot, plane_peer), (gx, line_peer)
            self.who = [(core, core_peer)] + ([along, across] if which == 0 else [across, along])
            self.flights = []

        def fly(self, level, slot, src, dst, step):
            copy = pltpu.make_async_remote_copy(
                src_ref=src, dst_ref=dst, send_sem=self.sends[level].at[slot],
                recv_sem=self.recvs[level].at[slot], device_id=self.who[level][1](step),
                device_id_type=MESH,
            )
            copy.start()
            self.flights.append(copy)

        def fill(self, level, used):
            peers, share = self.stages[level]
            if peers * share > used:
                self.sums[level][used:] = jnp.zeros((peers * share - used, 8, 2 * chans), F32)

        def give(self, level):
            peers, share = self.stages[level]
            for step in range(1, peers):
                other = lax.rem(self.who[level][0] + step, peers)
                self.fly(level, step - 1, self.sums[level].at[pl.ds(other * share, share)],
                         self.ins[level].at[step - 1], step)

        def take(self, level):
            peers, share = self.stages[level]
            acc = self.sums[level][pl.ds(self.who[level][0] * share, share)]
            for step, copy in enumerate(self.flights):
                copy.wait()
                acc = acc + self.ins[level][step]
            self.flights = []
            if level < 2:
                self.sums[level + 1][:share] = acc
                self.fill(level + 1, share)
            else:
                self.outs[2][pl.ds(self.who[2][0] * share, share)] = acc * scale

        def give_back(self, level):
            peers, share = self.stages[level]
            here = pl.ds(self.who[level][0] * share, share)
            src = self.outs[level].at[here] if level == 2 else self.outs[level + 1].at[pl.ds(0, share)]
            for step in range(1, peers):
                self.fly(level, peers + step - 2, src, self.outs[level].at[here], step)
            if level < 2:
                self.outs[level][here] = self.outs[level + 1][:share]

        def take_back(self):
            for copy in self.flights:
                copy.wait()
            self.flights = []

    early, late = Stream(0), Stream(1)
    for a in (-1, 0, 1):
        weight_term(a, 0, early.sums[0], 3 * (a + 1))
    early.fill(0, early.tiles)
    early.give(0)
    finish()
    cols[:, 0] = columns(pad[:, 0])
    cols[:, sy + 1] = columns(pad[:, sy + 1])
    for a in (-1, 0, 1):
        weight_term(a, -1, late.sums[0], 3 * (a + 1))
    early.take(0)
    early.give(1)
    for a in (-1, 0, 1):
        weight_term(a, 1, late.sums[0], 9 + 3 * (a + 1))
    late.fill(0, late.tiles)
    late.give(0)

    def input_rows(x):
        wide_cols, kernels = [], []
        for a in (-1, 0, 1):
            for b in (-1, 0, 1):
                rows = cols[x + 1 - a, 1 - b : 1 - b + sy].reshape(sy * sz, 4 * chans)
                k = 9 * (a + 1) + 3 * (b + 1)
                wide_cols.append(rows[:, : 3 * chans])
                kernels.append(w_ref[:, k * chans : (k + 3) * chans])
        total = jnp.zeros((sy * sz, chans), F32)
        for rows, kern in zip(wide_cols, kernels):
            total = total + lax.dot_general(
                rows, kern, (((1,), (1,)), ((), ())), preferred_element_type=F32
            )
        keep = mask[x * sy * sz : (x + 1) * sy * sz] > 0
        gi_ref[x] = jnp.where(keep, total, 0.0).astype(BF16).reshape(sy, sz, chans)

    loads[4].wait()
    late.take(0)
    late.give(1)
    for x in range(sx // 2):
        input_rows(x)
    early.take(1)
    early.give(2)
    for x in range(sx // 2, sx):
        input_rows(x)
    late.take(1)
    late.give(2)
    early.take(2)
    early.give_back(2)
    late.take(2)
    late.give_back(2)
    early.take_back()
    early.give_back(1)
    late.take_back()
    late.give_back(1)
    early.take_back()
    early.give_back(0)
    late.take_back()
    late.give_back(0)
    early.take_back()
    late.take_back()

    def block(k):
        a, b, e = k // 9, k // 3 % 3, k % 3
        full = early.outs[0] if b == 1 else late.outs[0]
        place = (0 if b < 2 else 9) + 3 * a + e
        return full[place * per : (place + 1) * per].reshape(half, 2 * chans)

    low = iota((half, 2 * chans), 1) < chans
    for k in range(0, 27, 2):
        one = block(k)
        if k == 26:
            gw_ref[:half, k * chans :] = one[:, :chans]
            gw_ref[half:, k * chans :] = pltpu.roll(one, chans, 1)[:, :chans]
            continue
        two = block(k + 1)
        at_k = slice(k * chans, (k + 2) * chans)
        gw_ref[:half, at_k] = jnp.where(low, one, pltpu.roll(two, chans, 1))
        gw_ref[half:, at_k] = jnp.where(low, pltpu.roll(one, chans, 1), two)


def local(sizes, grad_out, features, brick_mask, voxel_mask, weight):
    chans, sx, sy, sz = grad_out.shape
    n_gx, n_gy, n_gz = sizes
    cores, plane, streams = plan(sizes, chans)
    scale = 1.0 / math.sqrt(sx * sy * sz * n_gx * n_gy * n_gz)
    vmem = pl.BlockSpec(memory_space=pltpu.VMEM)
    dma = lambda n: pltpu.SemaphoreType.DMA((max(n, 1),))
    hbm = pl.BlockSpec(memory_space=pltpu.HBM)
    tile = (8, 2 * chans)
    stream_refs = []
    for _, stages in streams:
        whole = [pltpu.VMEM((peers * share, *tile), F32) for peers, share in stages]
        ins = [pltpu.VMEM((max(peers - 1, 1), share, *tile), F32) for peers, share in stages]
        sems = [dma(2 * (peers - 1)) for peers, _ in stages]
        stream_refs += whole + ins + whole + sems + sems
    grad_input, grad_weight = pl.pallas_call(
        functools.partial(kernel, sizes, scale),
        out_shape=(
            jax.ShapeDtypeStruct((sx, sy, sz, chans), BF16),
            jax.ShapeDtypeStruct((chans, 27 * chans), F32),
        ),
        in_specs=[hbm] * 5,
        out_specs=(vmem, vmem),
        scratch_shapes=[
            pltpu.VMEM((sx, sy, sz, chans), BF16),
            pltpu.VMEM((sx, sy, sz, chans), BF16),
            pltpu.SMEM(brick_mask.shape, jnp.int32),
            pltpu.VMEM((sx, sy, sz), jnp.int32),
            pltpu.VMEM(weight.shape, BF16),
            dma(5),
            pltpu.VMEM((sx + 2, sy + 2, sz, 2 * chans), BF16),
            pltpu.VMEM((sx + 2, sy + 2, sz, 4 * chans), BF16),
            pltpu.VMEM((sx * sy * sz, chans), F32),
            pltpu.VMEM((2 * sx * sy, 2 * chans), BF16),
            pltpu.VMEM((2 * sx * sy, 2 * chans), BF16),
            dma(6), dma(6), *stream_refs,
        ],
        compiler_params=pltpu.CompilerParams(
            collective_id=0, has_side_effects=True, vmem_limit_bytes=40 * 1024 * 1024
        ),
    )(
        jnp.transpose(grad_out, (1, 2, 3, 0)),
        jnp.transpose(features, (1, 2, 3, 0)),
        brick_mask,
        voxel_mask,
        weight,
    )
    return jnp.transpose(grad_input, (3, 0, 1, 2)), grad_weight


def solution(mesh):
    sizes = tuple(mesh.shape[name] for name in ("gx", "gy", "gz"))
    return jax.shard_map(
        functools.partial(local, sizes),
        mesh=mesh,
        in_specs=(
            P(None, "gx", "gy", "gz"),
            P(None, "gx", "gy", "gz"),
            P("gx", "gy", "gz"),
            P("gx", "gy", "gz"),
            P(),
        ),
        out_specs=(P(None, "gx", "gy", "gz"), P()),
        check_vma=False,
    )
```

time: 40 us -> 39.1 us (0.978)
  Pallas kernels: 33.4 us -> 32.5 us
    pallas_call x1, Pallas kernels: 33.4 us -> 32.5 us  [local(): pl.pallas_call(functools.partial(kernel, sizes, scale), out_shape=(jax.Sh...]
where the time goes in v2:
time: 39.1 us; the launch traced here: 38.8 us
  Pallas kernels  32.5 us (83%)
  local copies, waits for them, and re-layouts  5.71 us (15%)
  between operations  0.65 us (2%)
    pallas_call x1, Pallas kernels, local(): pl.pallas_call(functools.partial(kernel, sizes, scale), out_shape=(jax.Sh...  32.5 us
    unnamed x12, local copies, waits for them, and re-layouts  5.71 us

profile of v2, /device:TPU:0, one launch (start us, length us, event | category | flops | bytes accessed | tf_op | source)
XLA Modules:
  0.0 38.8 jit_solution(10136677322639512286)
XLA Ops:
  0.6 0.0 copy-start.4
  0.6 0.6 %copy-done.4 = s32[1,1,2]{2,1,0:T(1,128)S(1)} copy-done((s32[1,1,2]{2,1,0:T(1,128)S(1)}, s32[1,1,2]{2,1,0:T(1,128)}, u32[]{:S(2)}) %copy-start.4) | copy-done | bytes 32
  1.3 0.0 copy-start
  1.3 0.9 %copy-done = bf16[64,8,8,16]{0,3,2,1:T(8,128)(2,1)S(1)} copy-done((bf16[64,8,8,16]{0,3,2,1:T(8,128)(2,1)S(1)}, bf16[64,8,8,16]{0,3,2,1:T(8,128)(2,1)}, u32[]{:S(2)}) %copy-start) | copy-done | bytes 131096
  2.2 0.0 copy-start.1
  2.2 0.9 %copy-done.1 = bf16[64,8,8,16]{0,3,2,1:T(8,128)(2,1)S(1)} copy-done((bf16[64,8,8,16]{0,3,2,1:T(8,128)(2,1)S(1)}, bf16[64,8,8,16]{0,3,2,1:T(8,128)(2,1)}, u32[]{:S(2)}) %copy-start.1) | copy-done | bytes 131096
  3.2 0.0 copy-start.2
  3.2 0.9 %copy-done.2 = bf16[64,1728]{1,0:T(8,128)(2,1)S(1)} copy-done((bf16[64,1728]{1,0:T(8,128)(2,1)S(1)}, bf16[64,1728]{1,0:T(8,128)(2,1)}, u32[]{:S(2)}) %copy-start.2) | copy-done | bytes 221208
  4.1 0.0 copy-start.3
  4.1 0.8 %copy-done.3 = s32[8,8,16]{2,1,0:T(8,128)S(1)} copy-done((s32[8,8,16]{2,1,0:T(8,128)S(1)}, s32[8,8,16]{2,1,0:T(8,128)}, u32[]{:S(2)}) %copy-start.3) | copy-done | bytes 4120
  4.9 32.5 %shard_map.68 = (bf16[8,8,16,64]{3,2,1,0:T(8,128)(2,1)S(1)}, f32[64,1728]{1,0:T(8,128)S(1)}) custom-call(bf16[8,8,16,64]{3,2,1,0:T(8,128)(2,1)S(1)} %bitcast.4, bf16[8,8,16,64]{3,2,1,0:T(8,128)(2,1)S(1)} %bitcast.5, s32[1,1,2]{2,1,0:T(1,128)S(1)} %copy-done.4, s32[8,8,16]{2,1,0:T(8,128)S(1)} %copy-done.3, bf16[64,1728]{1,0:T(8,128)(2,1)S(1)} %copy-done.2), custom_call_target="tpu_custom_call" | custom-call | tf_op jit(solution)/shard_map/pallas_call | solution.py:376
  37.4 0.7 %copy.9 = bf16[64,8,8,16]{0,3,2,1:T(8,128)(2,1)} copy(bf16[64,8,8,16]{0,3,2,1:T(8,128)(2,1)S(1)} %bitcast.3) | data formatting | bytes 262144
  38.1 0.8 %copy.10 = f32[64,1728]{1,0:T(8,128)} copy(f32[64,1728]{1,0:T(8,128)S(1)} %get-tuple-element.9) | data formatting | bytes 884736
Async XLA Ops:
  0.6 0.7 %copy-start.4 = (s32[1,1,2]{2,1,0:T(1,128)S(1)}, s32[1,1,2]{2,1,0:T(1,128)}, u32[]{:S(2)}) copy-start(s32[1,1,2]{2,1,0:T(1,128)} %b_hbm.1) | copy-start | bytes 28
  1.3 0.9 %copy-start = (bf16[64,8,8,16]{0,3,2,1:T(8,128)(2,1)S(1)}, bf16[64,8,8,16]{0,3,2,1:T(8,128)(2,1)}, u32[]{:S(2)}) copy-start(bf16[64,8,8,16]{0,3,2,1:T(8,128)(2,1)} %param.5) | copy-start | bytes 393220
  2.2 0.9 %copy-start.1 = (bf16[64,8,8,16]{0,3,2,1:T(8,128)(2,1)S(1)}, bf16[64,8,8,16]{0,3,2,1:T(8,128)(2,1)}, u32[]{:S(2)}) copy-start(bf16[64,8,8,16]{0,3,2,1:T(8,128)(2,1)} %param.6) | copy-start | bytes 393220
  3.2 0.9 %copy-start.2 = (bf16[64,1728]{1,0:T(8,128)(2,1)S(1)}, bf16[64,1728]{1,0:T(8,128)(2,1)}, u32[]{:S(2)}) copy-start(bf16[64,1728]{1,0:T(8,128)(2,1)} %w_hbm.1) | copy-start | bytes 663556
  4.1 0.8 %copy-start.3 = (s32[8,8,16]{2,1,0:T(8,128)S(1)}, s32[8,8,16]{2,1,0:T(8,128)}, u32[]{:S(2)}) copy-start(s32[8,8,16]{2,1,0:T(8,128)} %v_hbm.1) | copy-start | bytes 12292

commit v3 on v2

--- a/solution.py
+++ b/solution.py
@@ -396,7 +396,7 @@
             dma(6), dma(6), *stream_refs,
         ],
         compiler_params=pltpu.CompilerParams(
-            collective_id=0, has_side_effects=True, vmem_limit_bytes=40 * 1024 * 1024
+            collective_id=0, has_side_effects=True, vmem_limit_bytes=62 * 1024 * 1024
         ),
     )(
         jnp.transpose(grad_out, (1, 2, 3, 0)),

time: 39.1 us -> 36.2 us (0.926)
  local copies, waits for them, and re-layouts: 5.71 us -> 2.5 us
  Pallas kernels: 32.5 us -> 32.9 us
    unnamed x12 -> x4, local copies, waits for them, and re-layouts: 5.71 us -> 2.5 us
    pallas_call x1, Pallas kernels: 32.5 us -> 32.9 us  [local(): pl.pallas_call(functools.partial(kernel, sizes, scale), out_shape=(jax.Sh...]
where the time goes in v3:
time: 36.2 us; the launch traced here: 36 us
  Pallas kernels  32.9 us (91%)
  local copies, waits for them, and re-layouts  2.5 us (7%)
  between operations  0.65 us (2%)
    pallas_call x1, Pallas kernels, local(): pl.pallas_call(functools.partial(kernel, sizes, scale), out_shape=(jax.Sh...  32.9 us
    unnamed x4, local copies, waits for them, and re-layouts  2.5 us

profile of v3, /device:TPU:0, one launch (start us, length us, event | category | flops | bytes accessed | tf_op | source)
XLA Modules:
  0.0 36.0 jit_solution(1505477163861431269)
XLA Ops:
  0.6 32.9 %shard_map.68 = (bf16[8,8,16,64]{3,2,1,0:T(8,128)(2,1)}, f32[64,1728]{1,0:T(8,128)}) custom-call(bf16[8,8,16,64]{3,2,1,0:T(8,128)(2,1)} %bitcast.4, bf16[8,8,16,64]{3,2,1,0:T(8,128)(2,1)} %bitcast.5, s32[1,1,2]{2,1,0:T(1,128)} %b_hbm.1, s32[8,8,16]{2,1,0:T(8,128)} %v_hbm.1, bf16[64,1728]{1,0:T(8,128)(2,1)} %w_hbm.1), custom_call_target="tpu_custom_call" | custom-call | tf_op jit(solution)/shard_map/pallas_call | solution.py:376
  33.5 0.0 copy-start
  33.5 1.7 %copy.9 = bf16[64,8,8,16]{0,3,2,1:T(8,128)(2,1)} copy(bf16[64,8,8,16]{0,3,2,1:T(8,128)(2,1)} %bitcast.3) | data formatting | bytes 262144
  35.3 0.0 copy-done
  35.3 0.8 %copy.10 = f32[64,1728]{1,0:T(8,128)} copy(f32[64,1728]{1,0:T(8,128)S(1)} %copy-done) | data formatting | bytes 884736
Async XLA Ops:
  33.5 1.7 %copy-start = (f32[64,1728]{1,0:T(8,128)S(1)}, f32[64,1728]{1,0:T(8,128)}, u32[]{:S(2)}) copy-start(f32[64,1728]{1,0:T(8,128)} %get-tuple-element.9) | copy-start | bytes 1327108

commit v4 on v3

--- a/solution.py
+++ b/solution.py
@@ -19,17 +19,9 @@
 
 def plan(sizes, chans):
     n_gx, n_gy, n_gz = sizes
-    cores = 2 if n_gz % 2 == 0 else 1
-    plane = n_gy * (n_gz // cores)
+    plane = n_gy * n_gz
     tiles = 9 * chans * chans // 1024
-    streams = []
-    for count, order in ((tiles, (cores, n_gx, plane)), (2 * tiles, (cores, plane, n_gx))):
-        stages, left = [], count
-        for peers in order:
-            left = ceil_div(left, peers)
-            stages.append((peers, left))
-        streams.append((count, stages))
-    return cores, plane, streams
+    return plane, [(count, ceil_div(count, plane)) for count in (tiles, 2 * tiles)]
 
 
 def div(x, n):
@@ -52,7 +44,7 @@
     n_gx, n_gy, n_gz = sizes
     sx, sy, sz, chans = g_ref.shape
     nxy, count = sx * sy, sx * sy * sz
-    cores, plane, streams = plan(sizes, chans)
+    plane, streams = plan(sizes, chans)
     loads = [
         pltpu.make_async_copy(src, dst, load_sem.at[i])
         for i, (src, dst) in enumerate(
@@ -62,25 +54,16 @@
     for load in loads:
         load.start()
     gx, gy, gz = lax.axis_index("gx"), lax.axis_index("gy"), lax.axis_index("gz")
-    core, xh = lax.rem(gz, cores), gz // cores
-    wide = n_gz // cores
-    spot = gy * wide + xh
+    spot = gy * n_gz + gz
 
     def plane_peer(step):
         other = lax.rem(spot + step, plane)
-        return (gx, other // wide, lax.rem(other, wide) * cores + core)
+        return (gx, other // n_gz, lax.rem(other, n_gz))
 
     def line_peer(step):
         return (lax.rem(gx + step, n_gx), gy, gz)
 
-    def core_peer(step):
-        return (gx, gy, xh * cores + lax.rem(core + step, cores))
-
     partners = [plane_peer(s) for s in range(1, plane)] + [line_peer(s) for s in range(1, n_gx)]
-    if cores == 2:
-        partners.append(core_peer(1))
-    if n_gz > cores:
-        partners.append((gx, gy, lax.rem(gz + n_gz + 2 * core - 1, n_gz)))
     barrier = pltpu.get_barrier_semaphore()
     for partner in partners:
         pl.semaphore_signal(barrier, inc=1, device_id=partner, device_id_type=MESH)
@@ -224,78 +207,68 @@
 
     class Stream:
         def __init__(self, which):
-            self.tiles, self.stages = streams[which]
-            refs = stream_refs[which * 15 : (which + 1) * 15]
-            self.sums, self.ins, self.outs = refs[0:3], refs[3:6], refs[6:9]
-            self.sends, self.recvs = refs[9:12], refs[12:15]
-            across, along = (spot, plane_peer), (gx, line_peer)
-            self.who = [(core, core_peer)] + ([along, across] if which == 0 else [across, along])
+            self.tiles, self.share = streams[which]
+            refs = stream_refs[which * 10 : (which + 1) * 10]
+            self.terms, self.got, self.line, self.out = refs[:4]
+            self.sems = refs[4:]
             self.flights = []
 
-        def fly(self, level, slot, src, dst, step):
+        def fly(self, stage, slot, src, dst, device):
             copy = pltpu.make_async_remote_copy(
-                src_ref=src, dst_ref=dst, send_sem=self.sends[level].at[slot],
-                recv_sem=self.recvs[level].at[slot], device_id=self.who[level][1](step),
+                src_ref=src, dst_ref=dst, send_sem=self.sems[2 * stage].at[slot],
+                recv_sem=self.sems[2 * stage + 1].at[slot], device_id=device,
                 device_id_type=MESH,
             )
             copy.start()
             self.flights.append(copy)
 
-        def fill(self, level, used):
-            peers, share = self.stages[level]
-            if peers * share > used:
-                self.sums[level][used:] = jnp.zeros((peers * share - used, 8, 2 * chans), F32)
-
-        def give(self, level):
-            peers, share = self.stages[level]
-            for step in range(1, peers):
-                other = lax.rem(self.who[level][0] + step, peers)
-                self.fly(level, step - 1, self.sums[level].at[pl.ds(other * share, share)],
-                         self.ins[level].at[step - 1], step)
-
-        def take(self, level):
-            peers, share = self.stages[level]
-            acc = self.sums[level][pl.ds(self.who[level][0] * share, share)]
+        def scatter(self):
+            if plane * self.share > self.tiles:
+                rest = plane * self.share - self.tiles
+                self.terms[self.tiles :] = jnp.zeros((rest, 8, 2 * chans), F32)
+            for step in range(1, plane):
+                other = lax.rem(spot + step, plane)
+                self.fly(0, step - 1, self.terms.at[pl.ds(other * self.share, self.share)],
+                         self.got.at[step - 1], plane_peer(step))
+
+        def exchange(self):
+            acc = self.terms[pl.ds(spot * self.share, self.share)]
             for step, copy in enumerate(self.flights):
                 copy.wait()
-                acc = acc + self.ins[level][step]
+                acc = acc + self.got[step]
             self.flights = []
-            if level < 2:
-                self.sums[level + 1][:share] = acc
-                self.fill(level + 1, share)
-            else:
-                self.outs[2][pl.ds(self.who[2][0] * share, share)] = acc * scale
-
-        def give_back(self, level):
-            peers, share = self.stages[level]
-            here = pl.ds(self.who[level][0] * share, share)
-            src = self.outs[level].at[here] if level == 2 else self.outs[level + 1].at[pl.ds(0, share)]
-            for step in range(1, peers):
-                self.fly(level, peers + step - 2, src, self.outs[level].at[here], step)
-            if level < 2:
-                self.outs[level][here] = self.outs[level + 1][:share]
-
-        def take_back(self):
+            self.line[gx] = acc
+            for step in range(1, n_gx):
+                self.fly(1, step - 1, self.line.at[gx], self.line.at[gx], line_peer(step))
+
+        def gather(self):
             for copy in self.flights:
                 copy.wait()
             self.flights = []
+            acc = self.line[0]
+            for i in range(1, n_gx):
+                acc = acc + self.line[i]
+            here = pl.ds(spot * self.share, self.share)
+            self.out[here] = acc * scale
+            for step in range(1, plane):
+                self.fly(2, step - 1, self.out.at[here], self.out.at[here], plane_peer(step))
+
+        def land(self):
+            for copy in self.flights:
+                copy.wait()
 
     early, late = Stream(0), Stream(1)
     for a in (-1, 0, 1):
-        weight_term(a, 0, early.sums[0], 3 * (a + 1))
-    early.fill(0, early.tiles)
-    early.give(0)
+        weight_term(a, 0, early.terms, 3 * (a + 1))
+    early.scatter()
     finish()
     cols[:, 0] = columns(pad[:, 0])
     cols[:, sy + 1] = columns(pad[:, sy + 1])
     for a in (-1, 0, 1):
-        weight_term(a, -1, late.sums[0], 3 * (a + 1))
-    early.take(0)
-    early.give(1)
+        weight_term(a, -1, late.terms, 3 * (a + 1))
     for a in (-1, 0, 1):
-        weight_term(a, 1, late.sums[0], 9 + 3 * (a + 1))
-    late.fill(0, late.tiles)
-    late.give(0)
+        weight_term(a, 1, late.terms, 9 + 3 * (a + 1))
+    late.scatter()
 
     def input_rows(x):
         wide_cols, kernels = [], []
@@ -314,34 +287,20 @@
         gi_ref[x] = jnp.where(keep, total, 0.0).astype(BF16).reshape(sy, sz, chans)
 
     loads[4].wait()
-    late.take(0)
-    late.give(1)
+    early.exchange()
     for x in range(sx // 2):
         input_rows(x)
-    early.take(1)
-    early.give(2)
+    late.exchange()
     for x in range(sx // 2, sx):
         input_rows(x)
-    late.take(1)
-    late.give(2)
-    early.take(2)
-    early.give_back(2)
-    late.take(2)
-    late.give_back(2)
-    early.take_back()
-    early.give_back(1)
-    late.take_back()
-    late.give_back(1)
-    early.take_back()
-    early.give_back(0)
-    late.take_back()
-    late.give_back(0)
-    early.take_back()
-    late.take_back()
+    early.gather()
+    late.gather()
+    early.land()
+    late.land()
 
     def block(k):
         a, b, e = k // 9, k // 3 % 3, k % 3
-        full = early.outs[0] if b == 1 else late.outs[0]
+        full = early.out if b == 1 else late.out
         place = (0 if b < 2 else 9) + 3 * a + e
         return full[place * per : (place + 1) * per].reshape(half, 2 * chans)
 
@@ -361,18 +320,21 @@
 def local(sizes, grad_out, features, brick_mask, voxel_mask, weight):
     chans, sx, sy, sz = grad_out.shape
     n_gx, n_gy, n_gz = sizes
-    cores, plane, streams = plan(sizes, chans)
+    plane, streams = plan(sizes, chans)
     scale = 1.0 / math.sqrt(sx * sy * sz * n_gx * n_gy * n_gz)
     vmem = pl.BlockSpec(memory_space=pltpu.VMEM)
     dma = lambda n: pltpu.SemaphoreType.DMA((max(n, 1),))
     hbm = pl.BlockSpec(memory_space=pltpu.HBM)
     tile = (8, 2 * chans)
     stream_refs = []
-    for _, stages in streams:
-        whole = [pltpu.VMEM((peers * share, *tile), F32) for peers, share in stages]
-        ins = [pltpu.VMEM((max(peers - 1, 1), share, *tile), F32) for peers, share in stages]
-        sems = [dma(2 * (peers - 1)) for peers, _ in stages]
-        stream_refs += whole + ins + whole + sems + sems
+    for _, share in streams:
+        stream_refs += [
+            pltpu.VMEM((plane * share, *tile), F32),
+            pltpu.VMEM((max(plane - 1, 1), share, *tile), F32),
+            pltpu.VMEM((n_gx, share, *tile), F32),
+            pltpu.VMEM((plane * share, *tile), F32),
+        ]
+        stream_refs += [dma(n - 1) for n in (plane, plane, n_gx, n_gx, plane, plane)]
     grad_input, grad_weight = pl.pallas_call(
         functools.partial(kernel, sizes, scale),
         out_shape=(

time: 36.2 us -> 34.1 us (0.942)
  Pallas kernels: 32.9 us -> 30.8 us
    pallas_call x1, Pallas kernels: 32.9 us -> 30.8 us  [local(): pl.pallas_call(functools.partial(kernel, sizes, scale), out_shape=(jax.Sh...]
where the time goes in v4:
time: 34.1 us; the launch traced here: 33.9 us
  Pallas kernels  30.8 us (90%)
  local copies, waits for them, and re-layouts  2.5 us (7%)
  between operations  0.65 us (2%)
    pallas_call x1, Pallas kernels, local(): pl.pallas_call(functools.partial(kernel, sizes, scale), out_shape=(jax.Sh...  30.8 us
    unnamed x4, local copies, waits for them, and re-layouts  2.5 us

profile of v4, /device:TPU:0, one launch (start us, length us, event | category | flops | bytes accessed | tf_op | source)
XLA Modules:
  0.0 33.9 jit_solution(10391828731642111667)
XLA Ops:
  0.6 30.8 %shard_map.68 = (bf16[8,8,16,64]{3,2,1,0:T(8,128)(2,1)}, f32[64,1728]{1,0:T(8,128)}) custom-call(bf16[8,8,16,64]{3,2,1,0:T(8,128)(2,1)} %bitcast.4, bf16[8,8,16,64]{3,2,1,0:T(8,128)(2,1)} %bitcast.5, s32[1,1,2]{2,1,0:T(1,128)} %b_hbm.1, s32[8,8,16]{2,1,0:T(8,128)} %v_hbm.1, bf16[64,1728]{1,0:T(8,128)(2,1)} %w_hbm.1), custom_call_target="tpu_custom_call" | custom-call | tf_op jit(solution)/shard_map/pallas_call | solution.py:338
  31.4 0.0 copy-start
  31.4 1.7 %copy.9 = bf16[64,8,8,16]{0,3,2,1:T(8,128)(2,1)} copy(bf16[64,8,8,16]{0,3,2,1:T(8,128)(2,1)} %bitcast.3) | data formatting | bytes 262144
  33.1 0.0 copy-done
  33.1 0.8 %copy.10 = f32[64,1728]{1,0:T(8,128)} copy(f32[64,1728]{1,0:T(8,128)S(1)} %copy-done) | data formatting | bytes 884736
Async XLA Ops:
  31.4 1.7 %copy-start = (f32[64,1728]{1,0:T(8,128)S(1)}, f32[64,1728]{1,0:T(8,128)}, u32[]{:S(2)}) copy-start(f32[64,1728]{1,0:T(8,128)} %get-tuple-element.9) | copy-start | bytes 1327108

commit v5 on v4

--- a/solution.py
+++ b/solution.py
@@ -64,6 +64,12 @@
         return (lax.rem(gx + step, n_gx), gy, gz)
 
     partners = [plane_peer(s) for s in range(1, plane)] + [line_peer(s) for s in range(1, n_gx)]
+    diagonals = [(dx, dy) for dx in (-1, 1) for dy in (-1, 1)]
+
+    def corner_peer(dx, dy):
+        return (lax.rem(gx + n_gx + dx, n_gx), lax.rem(gy + n_gy + dy, n_gy), gz)
+
+    partners += [corner_peer(dx, dy) for dx, dy in diagonals]
     barrier = pltpu.get_barrier_semaphore()
     for partner in partners:
         pl.semaphore_signal(barrier, inc=1, device_id=partner, device_id_type=MESH)
@@ -176,12 +182,46 @@
         2, gx, n_gx, lambda i: (i, gy, gz),
         pad.at[1, inner], pad.at[sx, inner], pad.at[0, inner], pad.at[sx + 1, inner],
     )
+    along_x = pl.ds(1, sx)
+    finish_y = swap(
+        4, gy, n_gy, lambda i: (gx, i, gz),
+        pad.at[along_x, 1], pad.at[along_x, sy], pad.at[along_x, 0], pad.at[along_x, sy + 1],
+    )
+
+    def corner(slot, dx, dy):
+        src = pad.at[sx if dx > 0 else 1, sy if dy > 0 else 1]
+        dst = pad.at[0 if dx > 0 else sx + 1, 0 if dy > 0 else sy + 1]
+        copy = lambda: pltpu.make_async_remote_copy(
+            src_ref=src, dst_ref=dst, send_sem=halo_send.at[6 + slot],
+            recv_sem=halo_recv.at[6 + slot], device_id=corner_peer(dx, dy), device_id_type=MESH,
+        )
+
+        def inside(sign):
+            x, y = gx + sign * dx, gy + sign * dy
+            return (x >= 0) & (x < n_gx) & (y >= 0) & (y < n_gy)
+
+        @pl.when(inside(1))
+        def _():
+            copy().start()
+
+        def finish_corner():
+            @pl.when(inside(-1))
+            def _():
+                copy().wait_recv()
+
+            @pl.when(jnp.logical_not(inside(-1)))
+            def _():
+                dst[...] = jnp.zeros(dst.shape, dst.dtype)
+
+            @pl.when(inside(1))
+            def _():
+                copy().wait_send()
+
+        return finish_corner
+
+    corners = [corner(slot, dx, dy) for slot, (dx, dy) in enumerate(diagonals)]
     cols[1 : sx + 1, 1 : sy + 1] = columns(pad[1 : sx + 1, 1 : sy + 1])
     finish()
-    finish = swap(
-        4, gy, n_gy, lambda i: (gx, i, gz),
-        pad.at[:, 1], pad.at[:, sy], pad.at[:, 0], pad.at[:, sy + 1],
-    )
     cols[0, 1 : sy + 1] = columns(pad[0, 1 : sy + 1])
     cols[sx + 1, 1 : sy + 1] = columns(pad[sx + 1, 1 : sy + 1])
 
@@ -261,7 +301,9 @@
     for a in (-1, 0, 1):
         weight_term(a, 0, early.terms, 3 * (a + 1))
     early.scatter()
-    finish()
+    finish_y()
+    for finish_corner in corners:
+        finish_corner()
     cols[:, 0] = columns(pad[:, 0])
     cols[:, sy + 1] = columns(pad[:, sy + 1])
     for a in (-1, 0, 1):
@@ -338,8 +380,8 @@
     grad_input, grad_weight = pl.pallas_call(
         functools.partial(kernel, sizes, scale),
         out_shape=(
-            jax.ShapeDtypeStruct((sx, sy, sz, chans), BF16),
-            jax.ShapeDtypeStruct((chans, 27 * chans), F32),
+            pltpu.VMEM((sx, sy, sz, chans), BF16),
+            pltpu.VMEM((chans, 27 * chans), F32),
         ),
         in_specs=[hbm] * 5,
         out_specs=(vmem, vmem),
@@ -355,10 +397,10 @@
             pltpu.VMEM((sx * sy * sz, chans), F32),
             pltpu.VMEM((2 * sx * sy, 2 * chans), BF16),
             pltpu.VMEM((2 * sx * sy, 2 * chans), BF16),
-            dma(6), dma(6), *stream_refs,
+            dma(10), dma(10), *stream_refs,
         ],
         compiler_params=pltpu.CompilerParams(
-            collective_id=0, has_side_effects=True, vmem_limit_bytes=62 * 1024 * 1024
+            collective_id=0, has_side_effects=True, vmem_limit_bytes=60 * 1024 * 1024
         ),
     )(
         jnp.transpose(grad_out, (1, 2, 3, 0)),

time: 34.1 us -> 30.2 us (0.89)
  Pallas kernels: 30.8 us -> 28 us
  local copies, waits for them, and re-layouts: 2.5 us -> 1.47 us
    pallas_call x1, Pallas kernels: 30.8 us -> 28 us  [local(): pl.pallas_call(functools.partial(kernel, sizes, scale), out_shape=(pltpu....]
    unnamed x4 -> x2, local copies, waits for them, and re-layouts: 2.5 us -> 1.47 us
where the time goes in v5:
time: 30.2 us; the launch traced here: 30.1 us
  Pallas kernels  28 us (93%)
  local copies, waits for them, and re-layouts  1.47 us (5%)
  between operations  0.64 us (2%)
    pallas_call x1, Pallas kernels, local(): pl.pallas_call(functools.partial(kernel, sizes, scale), out_shape=(pltpu....  28 us
    unnamed x2, local copies, waits for them, and re-layouts  1.47 us

profile of v5, /device:TPU:0, one launch (start us, length us, event | category | flops | bytes accessed | tf_op | source)
XLA Modules:
  0.0 30.1 jit_solution(5939095619645236763)
XLA Ops:
  0.6 28.0 %shard_map.68 = (bf16[8,8,16,64]{3,2,1,0:T(8,128)(2,1)S(1)}, f32[64,1728]{1,0:T(8,128)S(1)}) custom-call(bf16[8,8,16,64]{3,2,1,0:T(8,128)(2,1)} %bitcast.4, bf16[8,8,16,64]{3,2,1,0:T(8,128)(2,1)} %bitcast.5, s32[1,1,2]{2,1,0:T(1,128)} %b_hbm.1, s32[8,8,16]{2,1,0:T(8,128)} %v_hbm.1, bf16[64,1728]{1,0:T(8,128)(2,1)} %w_hbm.1), custom_call_target="tpu_custom_call" | custom-call | tf_op jit(solution)/shard_map/pallas_call | solution.py:380
  28.6 0.7 %copy.9 = bf16[64,8,8,16]{0,3,2,1:T(8,128)(2,1)} copy(bf16[64,8,8,16]{0,3,2,1:T(8,128)(2,1)S(1)} %bitcast.3) | data formatting | bytes 262144
  29.3 0.8 %copy.10 = f32[64,1728]{1,0:T(8,128)} copy(f32[64,1728]{1,0:T(8,128)S(1)} %get-tuple-element.7) | data formatting | bytes 884736
